TPU v7x, 256 devices: a whole 4x4x8 slice. The times are simulated.
256 devices in a mesh: chan: 32 (over y, z_lo, x), tm: 8 (over z_hi, core).
Axes of the slice: x: 4, y: 4, z: 8 (z_hi: 4, z_lo: 2; z = z_hi * 2 + z_lo), core: 2. Of those that a mesh axis runs over, the one named last changes fastest.
Arguments:
- record: bfloat16 [8, 1024, 7680], P('tm', None, 'chan'), may hold values from -6 to 6
- fir_taps: bfloat16 [257], replicated, may hold values from -0.375 to 0.375
- sources: int32 [64], replicated, may hold values from 0 to 1023, as said below
- valid_mask: int32 [8, 1024], replicated, may hold values 0 or 1
Outputs:
- stack: float32 [64, 1024, 512], P('tm', 'chan')
Inputs may be any that keep to these rules, and one draw needn't show every extreme that they name: `sources`: source s is one of the channels s * 16 to (s + 1) * 16 - 1; source 0 is channel 0 and the last source is the last channel.
All inputs are finite; a program needn't handle non-finite values.
Results may differ from a plain program's by a relative error of at most 0.011.
Values may be sent and summed in bfloat16 or wider, within the bound.
No kernel may reach another device: no remote copies, remote signals or barrier semaphores. Data moves between devices by JAX's collectives and lax.ppermute only.
A program may use at most 64 MiB of HBM per device.

v0:
```python
import functools
import math

import jax
import jax.numpy as jnp
import numpy as np
from jax import lax
from jax.experimental import pallas as pl
from jax.experimental.pallas import tpu as pltpu
from jax.sharding import PartitionSpec as P

SPAN = 8192
SAMPLES = 7680
ROWS_B = 32
COLS_A = 256
HALF = 128
BAND = 128
MAXLAG = 256
LAGS = 512
TILE = 256
STEP_K2 = 16
ROW_STEP = 16
ROW_PART = 8
VMEM_LIMIT = 16 * 1024 * 1024
PLANES = ROWS_B + 1


def angle_tables(left, right, period):
    angles = (np.outer(left, right) % period) * (2.0 * math.pi / period)
    return np.cos(angles), np.sin(angles)


@functools.cache
def tables():
    b = np.arange(ROWS_B)
    a = np.arange(COLS_A)
    k1 = np.arange(HALF)
    cos_b, sin_b = angle_tables(b, b, ROWS_B)
    used = np.concatenate([cos_b, -sin_b], axis=0)[:, : SAMPLES // COLS_A]
    first = np.kron(used, np.eye(ROW_PART))
    twist = np.stack(angle_tables(b, a, SPAN)).astype(np.float32)
    cos_a, sin_a = angle_tables(a, k1, COLS_A)
    second = np.concatenate(
        [np.concatenate([cos_a, -sin_a], axis=1), np.concatenate([sin_a, cos_a], axis=1)], axis=0
    )
    bins = b[:, None] + ROWS_B * k1[None, :]
    shift = np.stack([np.cos(bins * math.pi / SPAN), np.sin(bins * math.pi / SPAN)])
    odd = 2 * np.arange(MAXLAG) + 1
    angles = (np.outer(bins.reshape(-1), odd) % (2 * SPAN)) * (math.pi / SPAN)
    scale = 1.0 / math.sqrt(SPAN)
    lag_cos = (np.cos(angles) * scale).reshape(ROWS_B, HALF, MAXLAG)
    lag_sin = (np.sin(angles) * scale).reshape(ROWS_B, HALF, MAXLAG)
    lag_sin[0, 0] = scale * (1 - 2 * (np.arange(MAXLAG) % 2))
    band = k1 // 4
    same = (band[:, None] == band[None, :]).astype(np.float32)
    lead = (k1 % 4 == 0)[:, None]
    following = (k1[:, None] == 4 * (band[None, :] + 1)).astype(np.float32)
    mirror_rest, mirror_edge = same, same * ~lead + following
    back = np.where(k1 % 4 == 0, np.maximum(k1 - 1, 0), k1)
    sums = np.concatenate(
        [
            np.concatenate([same, mirror_rest, mirror_rest[:, back]], axis=1),
            np.concatenate([same, mirror_edge, mirror_edge[:, back]], axis=1),
        ],
        axis=0,
    )
    nyquist = np.zeros((1, 3 * HALF), np.float32)
    nyquist[0, HALF + 124 : 2 * HALF] = 1.0
    nyquist[0, 2 * HALF + 125 :] = 1.0
    signs = (1.0 - 2.0 * (np.arange(COLS_A) % 2))[None].astype(np.float32)
    bf16 = jnp.bfloat16
    return dict(
        turn=np.eye(MAXLAG)[::-1].astype(bf16),
        products=np.concatenate(
            [np.pad(first, ((0, 0), (0, COLS_A - first.shape[1]))), second, sums[:, : 2 * HALF]]
            + [np.pad(sums[:, 2 * HALF :], ((0, 0), (0, HALF)))]
        ).astype(bf16),
        rotations=np.concatenate(
            [twist[0], twist[1], np.concatenate([shift[0], shift[1]], axis=1)]
            + [np.repeat(v, 8, axis=0) for v in (signs, nyquist[:, : 2 * HALF])]
            + [np.repeat(np.pad(nyquist[:, 2 * HALF :], ((0, 0), (0, HALF))), 8, axis=0)]
        ).astype(np.float32),
        lags=np.stack([lag_cos, lag_sin], axis=1).astype(bf16),
    )


def in_hbm(array):
    return pltpu.with_memory_space_constraint(array, pltpu.HBM)


def in_vmem(array):
    return pltpu.with_memory_space_constraint(jnp.asarray(array), pltpu.VMEM)


def toeplitz_kernel(taps_ref, *rest):
    out_ref = rest[-1]
    rows, width = out_ref.shape
    base = jnp.broadcast_to(taps_ref[...], (rows, taps_ref.shape[1]))
    turned = pltpu.roll(base, taps_ref.shape[1] - MAXLAG, 1, stride=1, stride_axis=0)
    out_ref[...] = turned[:, :width].astype(out_ref.dtype)


def toeplitz_of(fir_taps, *held):
    base = jnp.pad(fir_taps.astype(jnp.float32), (0, 1024 - fir_taps.shape[0]))[None, :]
    return pl.pallas_call(
        toeplitz_kernel,
        in_specs=[pl.BlockSpec(base.shape, lambda: (0, 0))] + [pl.BlockSpec(memory_space=pl.ANY)] * len(held),
        out_shape=jax.ShapeDtypeStruct((2 * TILE, TILE), jnp.bfloat16),
        compiler_params=pltpu.CompilerParams(vmem_limit_bytes=VMEM_LIMIT),
        name="toeplitz",
    )(base, *held)


def gather_kernel(sources_ref, record_ref, out_ref, picked):
    sources = sources_ref.shape[1]
    count, rows, _ = out_ref.shape
    own = rows - sources
    step = pl.program_id(0)
    turned = (((1,), (1,)), ((), ()))

    def pick(rows_wanted, values):
        channel = lax.broadcasted_iota(jnp.int32, (rows_wanted.shape[0], values.shape[1]), 1)
        picker = jnp.where(channel == rows_wanted, 1.0, 0.0).astype(jnp.bfloat16)
        rows_of = lax.dot_general(picker, values, turned, preferred_element_type=jnp.float32)
        return rows_of.astype(jnp.bfloat16)

    @pl.when(step == 0)
    def _():
        order = source_order(lax.axis_index("tm"), (sources, sources))
        lane = lax.broadcasted_iota(jnp.int32, (sources, sources), 1)
        channels = jnp.where(lane == order, sources_ref[...].astype(jnp.float32), 0.0)
        channels = jnp.sum(channels, axis=1, keepdims=True).astype(jnp.int32)
        picked[...] = pick(channels, record_ref[...])

    here = pl.ds(pl.multiple_of(step * (count * own), count * own), count * own)
    straight = lax.broadcasted_iota(jnp.int32, (count * own, 1), 0)
    mine = pick(straight, record_ref[:, here])
    for i in range(count):
        out_ref[i, :sources] = picked[...]
        out_ref[i, sources:] = mine[i * own : (i + 1) * own]


def gather_rows(sources, record, chan_count):
    length, channels = record.shape
    total = sources.shape[0]
    rows = total + channels // chan_count
    steps = 2
    return pl.pallas_call(
        gather_kernel,
        grid=(steps,),
        in_specs=[
            pl.BlockSpec((1, total), lambda i: (0, 0)),
            pl.BlockSpec((length, channels), lambda i: (0, 0)),
        ],
        out_specs=pl.BlockSpec((chan_count // steps, rows, length), lambda i: (i, 0, 0)),
        out_shape=jax.ShapeDtypeStruct((chan_count, rows, length), jnp.bfloat16),
        scratch_shapes=[pltpu.VMEM((total, length), jnp.bfloat16)],
        compiler_params=pltpu.CompilerParams(vmem_limit_bytes=VMEM_LIMIT),
        name="gather",
    )(in_hbm(sources[None, :]), in_hbm(record))


def front_kernel(rotated, pieces_ref, toeplitz_ref, products_ref, rotations_ref, mask_ref, out_ref, signal):
    count, rows, part = pieces_ref.shape
    length = count * part
    f32, bf16 = jnp.float32, jnp.bfloat16
    signal[:, :HALF] = jnp.zeros((rows, HALF), bf16)
    signal[:, HALF + length :] = jnp.zeros((rows, HALF), bf16)
    for i in range(count):
        signal[:, HALF + i * part : HALF + (i + 1) * part] = pieces_ref[i]
    tiles = jnp.concatenate(
        [signal[:, n * TILE : n * TILE + 2 * TILE] for n in range(length // TILE)], axis=0
    )
    made = jnp.dot(tiles, toeplitz_ref[...], preferred_element_type=f32)
    made = made.reshape(length // TILE, rows, TILE)
    zetas = []
    split = 2 * ROWS_B * ROW_PART
    for part in range(rows // ROW_PART):
        filtered = made[:, part * ROW_PART : (part + 1) * ROW_PART].reshape(-1, TILE).astype(bf16)
        zetas.append(jnp.dot(products_ref[:split, : filtered.shape[0]], filtered, preferred_element_type=f32))
    turned_re, turned_im = [], []
    for k2 in range(ROWS_B):
        cos = jnp.broadcast_to(rotations_ref[k2 : k2 + 1, :], (ROW_PART, COLS_A))
        sin = jnp.broadcast_to(rotations_ref[ROWS_B + k2 : ROWS_B + k2 + 1, :], (ROW_PART, COLS_A))
        for zeta in zetas:
            zeta_re = zeta[k2 * ROW_PART : (k2 + 1) * ROW_PART]
            zeta_im = zeta[(ROWS_B + k2) * ROW_PART : (ROWS_B + k2 + 1) * ROW_PART]
            turned_re.append(zeta_re * cos + zeta_im * sin)
            turned_im.append(zeta_im * cos - zeta_re * sin)
    twisted_re = jnp.concatenate(turned_re, axis=0).astype(bf16)
    twisted_im = jnp.concatenate(turned_im, axis=0).astype(bf16)
    nyquist = jnp.sum(twisted_re[:rows].astype(f32) * rotations_ref[3 * ROWS_B : 3 * ROWS_B + 1], axis=1, keepdims=True)
    twisted = jnp.concatenate([twisted_re, twisted_im], axis=1)
    spectrum = jnp.dot(twisted, products_ref[split : split + 2 * COLS_A], preferred_element_type=f32)
    re, im = spectrum[:, :HALF], spectrum[:, HALF:]

    size = jnp.sqrt(re * re + im * im)
    rest = jnp.sum(size[rows:].reshape(ROWS_B - 1, rows, HALF), axis=0)
    both = jnp.concatenate([rest, size[:rows]], axis=1)
    high = both.astype(bf16)
    left = both - high.astype(f32)
    middle = left.astype(bf16)
    low = (left - middle.astype(f32)).astype(bf16)
    split += 2 * COLS_A
    parts = jnp.concatenate([high, middle, low], axis=0)
    parts = [
        jnp.dot(parts, products_ref[at : at + 2 * HALF], preferred_element_type=f32)
        for at in (split, split + 2 * HALF)
    ]
    parts = jnp.concatenate([parts[0], parts[1][:, :HALF]], axis=1)
    sums = parts[:rows] + parts[rows : 2 * rows] + parts[2 * rows :]
    at = 3 * ROWS_B + 8
    first_part, last_part = rotations_ref[at : at + 1], rotations_ref[at + 8 : at + 9, :HALF]
    sums = sums + jnp.abs(nyquist) * jnp.concatenate([first_part, last_part], axis=1)
    levels = sums * (1.0 / BAND) + 1e-05
    level, mirror, mirror_lead = levels[:, :HALF], levels[:, HALF : 2 * HALF], levels[:, 2 * HALF :]
    lane = lax.broadcasted_iota(jnp.int32, (rows, HALF), 1)
    mask = mask_ref[...]
    gain = mask / level
    white_nyquist = mask[:, :1] * nyquist / mirror[:, HALF - 1 :]
    ratio = (level / mirror).astype(bf16)
    ratio_lead = jnp.where(lane == 0, 0.0, level / mirror_lead).astype(bf16)

    def write(out_ref, rotate):
        for k2 in range(ROWS_B):
            here = slice(k2 * rows, (k2 + 1) * rows)
            white_re, white_im = re[here] * gain, im[here] * gain
            if rotate:
                turns = rotations_ref[2 * ROWS_B + k2 : 2 * ROWS_B + k2 + 1, :]
                turn_cos = jnp.broadcast_to(turns[:, :HALF], (rows, HALF))
                turn_sin = jnp.broadcast_to(turns[:, HALF:], (rows, HALF))
                white_re, white_im = (
                    white_re * turn_cos + white_im * turn_sin,
                    white_im * turn_cos - white_re * turn_sin,
                )
            if k2 == 0:
                white_im = jnp.where(lane == 0, white_nyquist, white_im)
            out_ref[k2, :, :HALF] = white_re.astype(bf16)
            out_ref[k2, :, HALF:] = white_im.astype(bf16)
        out_ref[ROWS_B, :, :HALF] = ratio
        out_ref[ROWS_B, :, HALF:] = ratio_lead

    is_source = pl.program_id(0) < rotated
    pl.when(is_source)(lambda: write(out_ref, True))
    pl.when(jnp.logical_not(is_source))(lambda: write(out_ref, False))


def front(pieces, toeplitz, products, rotations, mask, start, rows, rotated):
    count, _, part = pieces.shape
    start = start // ROW_STEP

    def whole(array):
        return pl.BlockSpec(array.shape, lambda i, rank=array.ndim: (0,) * rank)

    return pl.pallas_call(
        functools.partial(front_kernel, rotated // ROW_STEP),
        grid=(rows // ROW_STEP,),
        in_specs=[
            pl.BlockSpec((count, ROW_STEP, part), lambda i: (0, start + i, 0)),
            whole(toeplitz),
            whole(products),
            whole(rotations),
            pl.BlockSpec((ROW_STEP, HALF), lambda i: (start + i, 0)),
        ],
        out_specs=pl.BlockSpec((PLANES, ROW_STEP, 2 * HALF), lambda i: (0, i, 0)),
        out_shape=jax.ShapeDtypeStruct((PLANES, rows, 2 * HALF), jnp.bfloat16),
        scratch_shapes=[pltpu.VMEM((ROW_STEP, count * part + 2 * HALF), jnp.bfloat16)],
        compiler_params=pltpu.CompilerParams(vmem_limit_bytes=VMEM_LIMIT),
        cost_estimate=pl.CostEstimate(flops=rows * 110_000_000, bytes_accessed=4_000_000, transcendentals=0),
        name="front",
    )(in_vmem(pieces), in_vmem(toeplitz), products, rotations, mask)


def correlate_kernel(src0, src1, sratio0, sratio1, chan0, chan1, cratio0, cratio1, lags_ref, turn_ref,
                     *rest):
    outs, (even, odd, weight, lead_weight, src_wide) = rest[:-5], rest[-5:]
    step = pl.program_id(0)
    chans = chan0.shape[1]
    sources = src0.shape[1]
    f32, bf16 = jnp.float32, jnp.bfloat16
    srcs, chan_refs = (src0, src1), (chan0, chan1)

    def spread(w, j, s, h):
        return jnp.broadcast_to(src_wide[w, j, h, pl.ds(s, 1), :], (chans, HALF)).astype(bf16)

    @pl.when(step == 0)
    def _():
        for w, (sratio, cratio) in enumerate(((sratio0, cratio0), (sratio1, cratio1))):
            for h in range(2):
                src_wide[w, 0, h] = sratio[0, :, h * HALF : (h + 1) * HALF].astype(f32)
            for s in range(sources):
                weight[w, s] = 1.0 + cratio[0, :, :HALF] * spread(w, 0, s, 0)
                lead_weight[w, s] = 1.0 + cratio[0, :, HALF:] * spread(w, 0, s, 1)

    for w in range(2):
        for h in range(2):
            src_wide[w, :, h] = srcs[w][:, :, h * HALF : (h + 1) * HALF].astype(f32)

    def products(with_lead):
        parts_re, parts_im = [], []
        lane = lax.broadcasted_iota(jnp.int32, (chans, HALF), 1)
        keep = jnp.where(lane == 0, 0.0, 1.0).astype(bf16)
        only = jnp.where(lane == 0, 1.0, 0.0).astype(bf16)
        for s in range(sources):
            row_re, row_im = [], []
            for j in range(STEP_K2):
                total_re = total_im = None
                for w in range(2):
                    chan_re, chan_im = chan_refs[w][j, :, :HALF], chan_refs[w][j, :, HALF:]
                    src_re, src_im = spread(w, j, s, 0), spread(w, j, s, 1)
                    same_re, same_im = src_re * chan_re, src_im * chan_im
                    mixed = src_im * chan_re - src_re * chan_im
                    if with_lead and j == 0:
                        scale = lead_weight[w, s]
                        part_re = (same_re + same_im * keep) * scale
                        part_im = (mixed * keep - same_im * only) * scale
                    else:
                        scale = weight[w, s]
                        part_re = (same_re + same_im) * scale
                        part_im = mixed * scale
                    total_re = part_re if w == 0 else total_re + part_re
                    total_im = part_im if w == 0 else total_im + part_im
                row_re.append(total_re)
                row_im.append(total_im)
            parts_re.append(jnp.concatenate(row_re, axis=1))
            parts_im.append(jnp.concatenate(row_im, axis=1))
        table_cos = lags_ref[:, 0].reshape(STEP_K2 * HALF, MAXLAG)
        table_sin = lags_ref[:, 1].reshape(STEP_K2 * HALF, MAXLAG)
        whole_re = jnp.concatenate(parts_re, axis=0)
        whole_im = jnp.concatenate(parts_im, axis=0)
        return (
            jnp.dot(whole_re, table_cos, preferred_element_type=f32),
            jnp.dot(whole_im, table_sin, preferred_element_type=f32),
        )

    @pl.when(step == 0)
    def _():
        even[...], odd[...] = products(True)

    @pl.when(step > 0)
    def _():
        part_even, part_odd = products(False)
        even[...] += part_even
        odd[...] += part_odd

    @pl.when(step == pl.num_programs(0) - 1)
    def _():
        early = (even[...] + odd[...]).astype(bf16)
        early = jnp.dot(early, turn_ref[...], preferred_element_type=f32)
        late = even[...] - odd[...]
        rows = sources * chans // len(outs)
        for i, out in enumerate(outs):
            here = slice(i * rows, (i + 1) * rows)
            out[:, :MAXLAG] = early[here].astype(out.dtype)
            out[:, MAXLAG:] = late[here].astype(out.dtype)


def correlate(near, swap, got, lags, part, dtypes):
    tab = tables()
    sources, outs = 16, len(dtypes)
    count = near.shape[1]
    steps = ROWS_B // STEP_K2
    rows = count * sources
    src_spec = pl.BlockSpec((STEP_K2, sources, 2 * HALF), lambda i: (i, part, 0))
    src_ratio = pl.BlockSpec((1, sources, 2 * HALF), lambda i: (ROWS_B, part, 0))
    chan_spec = pl.BlockSpec((STEP_K2, count, 2 * HALF), lambda i: (i, 1, 0))
    chan_ratio = pl.BlockSpec((1, count, 2 * HALF), lambda i: (ROWS_B, 1, 0))
    table = pl.BlockSpec((STEP_K2, 2, HALF, MAXLAG), lambda i: (i, 0, 0, 0))
    out_spec = pl.BlockSpec((rows // outs, LAGS), lambda i: (0, 0))
    return pl.pallas_call(
        correlate_kernel,
        grid=(steps,),
        in_specs=[src_spec, src_spec, src_ratio, src_ratio, chan_spec, chan_spec, chan_ratio, chan_ratio]
        + [table, pl.BlockSpec((MAXLAG, MAXLAG), lambda i: (0, 0))],
        out_specs=[out_spec] * outs,
        out_shape=[jax.ShapeDtypeStruct((rows // outs, LAGS), dtype) for dtype in dtypes],
        scratch_shapes=[
            pltpu.VMEM((rows, MAXLAG), jnp.float32),
            pltpu.VMEM((rows, MAXLAG), jnp.float32),
            pltpu.VMEM((2, sources, count, HALF), jnp.bfloat16),
            pltpu.VMEM((2, sources, count, HALF), jnp.bfloat16),
            pltpu.VMEM((2, STEP_K2, 2, sources, HALF), jnp.float32),
        ],
        compiler_params=pltpu.CompilerParams(vmem_limit_bytes=VMEM_LIMIT),
        cost_estimate=pl.CostEstimate(
            flops=4 * rows * SPAN * MAXLAG, bytes_accessed=8 * 1024 * 1024, transcendentals=0
        ),
        name="correlate",
    )(near, got, near, got, swap, got, swap, got, lags, tab["turn"])


def finish_kernel(own_ref, first_ref, second_ref, count_ref, out_ref):
    for at in range(0, LAGS, HALF):
        here = slice(at, at + HALF)
        total = own_ref[:, here] + first_ref[:, here].astype(jnp.float32)
        out_ref[:, here] = (total + second_ref[:, here].astype(jnp.float32)) / count_ref[...]


def finish(own, first, second, count):
    return pl.pallas_call(
        finish_kernel,
        out_shape=jax.ShapeDtypeStruct(own.shape, jnp.float32),
        compiler_params=pltpu.CompilerParams(vmem_limit_bytes=VMEM_LIMIT),
        name="finish",
    )(own, first, second, count)


def source_order(time_index, shape):
    row = lax.broadcasted_iota(jnp.int32, shape, 0)
    place = (row // 8) % 4
    parity = (time_index % 2 + row // 32) % 2
    near_by = jnp.where((place == 1) == (parity == 0), 1, 3)
    relative = jnp.where(place == 0, 2, jnp.where(place == 3, 0, near_by))
    z_hi = (time_index // 2 + relative) % 4
    return (2 * z_hi + parity) * 8 + row % 8


def body(record, fir_taps, sources, valid_mask):
    chan_count = lax.axis_size("chan")
    time_count = lax.axis_size("tm")
    _, channels, part_len = record.shape
    chan_local = channels // chan_count
    source_total = sources.shape[0]
    chan_index = lax.axis_index("chan")
    time_index = lax.axis_index("tm")
    first_chan = chan_index * chan_local

    sent = gather_rows(sources, record[0].T, chan_count)
    pieces = lax.all_to_all(sent, "chan", split_axis=0, concat_axis=0, tiled=True)

    tab = tables()
    products, rotations = in_vmem(tab["products"]), in_vmem(tab["rotations"])
    lags = in_vmem(tab["lags"])
    toeplitz = toeplitz_of(fir_taps, products, rotations)
    valid_float = valid_mask.astype(jnp.float32)
    every_source = jnp.arange(source_total, dtype=jnp.int32)
    every_channel = jnp.arange(channels, dtype=jnp.int32)
    order = source_order(time_index, (source_total, 1))
    ordered = jnp.sum(jnp.where(order == every_source[None, :], sources[None, :], 0), axis=1)
    own = first_chan + jnp.arange(chan_local, dtype=jnp.int32)
    rows = jnp.concatenate([ordered, own])
    window_valid = lax.dynamic_index_in_dim(valid_float, time_index, 0, keepdims=False)
    mask = jnp.sum(jnp.where(rows[:, None] == every_channel[None, :], window_valid[None, :], 0.0), axis=1)
    mask = jnp.broadcast_to(mask[:, None], (rows.shape[0], HALF))
    chan_valid = lax.dynamic_slice_in_dim(valid_float, first_chan, chan_local, 1)
    rows_out = source_total // time_count
    own_sources = lax.dynamic_slice_in_dim(sources, time_index * rows_out, rows_out, 0)
    own_picker = (own_sources[:, None] == every_channel[None, :]).astype(jnp.float32)
    own_valid = jnp.dot(own_picker, valid_float.T, precision=lax.Precision.HIGHEST)
    pair_count = jnp.dot(own_valid, chan_valid, precision=lax.Precision.HIGHEST)

    third = source_total // 2
    swap = front(pieces, toeplitz, products, rotations, mask, third, 2 * third, third)
    got = lax.ppermute(swap, "tm", [(j, j ^ 1) for j in range(time_count)])
    near = front(pieces, toeplitz, products, rotations, mask, 0, third, third)

    def along(way, values):
        steps = [2 * way * (1 - 2 * (j % 2)) for j in range(time_count)]
        return lax.ppermute(values, "tm", [(j, (j + steps[j]) % time_count) for j in range(time_count)])

    bf16, f32 = jnp.bfloat16, jnp.float32
    far, first = correlate(near, swap, got, lags, 0, (bf16, f32))
    far = along(1, far)
    second, own_part = correlate(near, swap, got, lags, 1, (bf16, f32))
    first = along(1, (first + far.astype(f32)).astype(bf16))
    second = along(-1, second)
    count = jnp.maximum(pair_count, 1.0)[:, :, None]
    count = jnp.broadcast_to(count, count.shape[:2] + (HALF,)).reshape(rows_out * chan_local, HALF)
    stack = finish(own_part, first, second, count)
    return stack.reshape(rows_out, chan_local, LAGS)


def solution(mesh):
    return jax.shard_map(
        body,
        mesh=mesh,
        in_specs=(P("tm", None, "chan"), P(), P(), P()),
        out_specs=P("tm", "chan", None),
        check_vma=False,
    )
```

profile of v0, /device:TPU:1, one launch (start us, length us, event | category | flops | bytes accessed | tf_op | source)
XLA Modules:
  0.0 76.4 jit_solution(5593910806764210573)
XLA Ops:
  0.0 3.0 %gather.1 = bf16[32,96,240]{2,1,0:T(8,128)(2,1)} custom-call(s32[1,64]{1,0:T(1,128)} %bitcast.11, bf16[240,1024]{1,0:T(8,128)(2,1)} %bitcast.9), custom_call_target="tpu_custom_call" | custom-call | tf_op jit(solution)/shard_map/gather/pallas_call | solution.py:148
  3.0 0.0 copy-start.4
  3.0 0.0 copy-start.5
  3.0 0.0 copy-start
  3.0 0.0 copy-start.1
  3.0 0.0 copy-start.6
  3.0 9.4 %all-to-all-start = ((bf16[32,96,240]{2,1,0:T(8,128)(2,1)}), bf16[32,96,240]{2,1,0:T(8,128)(2,1)S(1)}, u32[]{:S(2)}, u32[]{:S(2)}) async-start(bf16[32,96,240]{2,1,0:T(8,128)(2,1)} %gather.1), calls=%async_computation | async-start | bytes 3145728 | tf_op jit(solution)/shard_map/all_to_all | solution.py:429
  12.4 0.0 copy-done.4
  12.4 0.0 copy-done.5
  12.5 0.0 copy-done
  12.5 0.0 copy-done.1
  12.5 0.1 toeplitz.1.toeplitz_ref
  12.6 0.0 copy-done.6
  12.7 0.2 select_reduce_fusion.1
  12.8 0.1 pad_add_fusion
  12.9 0.2 select_reduce_fusion
  13.1 20.1 %all-to-all-done.pieces_ref = bf16[32,96,240]{2,1,0:T(8,128)(2,1)S(1)} async-done(((bf16[32,96,240]{2,1,0:T(8,128)(2,1)}), bf16[32,96,240]{2,1,0:T(8,128)(2,1)S(1)}, u32[]{:S(2)}, u32[]{:S(2)}) %all-to-all-start) | async-done | bytes 1474592 | tf_op jit(solution)/shard_map/all_to_all | solution.py:429
  33.2 0.1 broadcast_in_dim.73.mask_ref
  33.3 6.5 %front.3.chan0.cratio0 = bf16[33,64,256]{2,1,0:T(8,128)(2,1)} custom-call(bf16[32,96,240]{2,1,0:T(8,128)(2,1)S(1)} %all-to-all-done.pieces_ref, bf16[512,256]{1,0:T(8,128)(2,1)S(1)} %toeplitz.1.toeplitz_ref, bf16[1536,256]{1,0:T(8,128)(2,1)S(1)} %copy-done, f32[120,256]{1,0:T(8,128)S(1)} %copy-done.1, f32[96,128]{1,0:T(8,128)S(1)} %broadcast_in_dim.73.mask_ref), custom_call_target="tpu_custom_call" | custom-call | flops 7040000000 | bytes 4000000 | tf_op jit(solution)/shard_map/front/pallas_call | solution.py:255
  39.8 2.2 %collective-permute-start = (bf16[33,64,256]{2,1,0:T(8,128)(2,1)}, bf16[33,64,256]{2,1,0:T(8,128)(2,1)}, u32[]{:S(2)}, u32[]{:S(2)}) collective-permute-start(bf16[33,64,256]{2,1,0:T(8,128)(2,1)} %front.3.chan0.cratio0), channel_id=1, source_target_pairs={{0,1},{1,0},{2,3},{3,2},{4,5},{5,4},{6,7},{7,6},{8,9},{9,8},{10,11... | collective-permute-start | bytes 3244040 | tf_op jit(solution)/shard_map/ppermute | solution.py:454
  42.0 0.1 dynamic_slice.11
  42.1 0.0 copy-start.2
  42.1 0.0 copy-start.3
  42.1 2.9 %front.2.src0.sratio0 = bf16[33,32,256]{2,1,0:T(8,128)(2,1)S(1)} custom-call(bf16[32,96,240]{2,1,0:T(8,128)(2,1)S(1)} %all-to-all-done.pieces_ref, bf16[512,256]{1,0:T(8,128)(2,1)S(1)} %toeplitz.1.toeplitz_ref, bf16[1536,256]{1,0:T(8,128)(2,1)S(1)} %copy-done, f32[120,256]{1,0:T(8,128)S(1)} %copy-done.1, f32[96,128]{1,0:T(8,128)S(1)} %broadcast_in_dim.73.mask_ref), custom_call_target="tpu_custom_call" | custom-call | flops 3520000000 | bytes 4000000 | tf_op jit(solution)/shard_map/front/pallas_call | solution.py:255
  45.0 0.0 collective-permute-done.src1.sratio1.chan1.cratio1
  45.0 0.0 copy-done.2
  45.0 0.0 copy-done.3
  45.0 4.7 %correlate.3 = (bf16[256,512]{1,0:T(8,128)(2,1)S(1)}, f32[256,512]{1,0:T(8,128)S(1)}) custom-call(bf16[33,32,256]{2,1,0:T(8,128)(2,1)S(1)} %front.2.src0.sratio0, bf16[33,64,256]{2,1,0:T(8,128)(2,1)} %collective-permute-done.src1.sratio1.chan1.cratio1, bf16[33,32,256]{2,1,0:T(8,128)(2,1)S(1)} %front.2.src0.sratio0, ...), custom_call_target="tpu_custom_call" | custom-call | flops 4294967296 | bytes 8388608 | tf_op jit(solution)/shard_map/correlate/pallas_call | solution.py:370
  49.8 5.2 %collective-permute-start.1 = (bf16[256,512]{1,0:T(8,128)(2,1)S(1)}, bf16[256,512]{1,0:T(8,128)(2,1)S(1)}, u32[]{:S(2)}, u32[]{:S(2)}) collective-permute-start(bf16[256,512]{1,0:T(8,128)(2,1)S(1)} %get-tuple-element.11), channel_id=1, source_target_pairs={{0,2},{1,7},{2,4},{3,1},{4,6},{5,3},{6,0},{7,5},{8,10},{9,15},{10,... | collective-permute-start | bytes 786440 | tf_op jit(solution)/shard_map/ppermute | solution.py:459
  55.0 4.7 %correlate.2 = (bf16[256,512]{1,0:T(8,128)(2,1)S(1)}, f32[256,512]{1,0:T(8,128)S(1)}) custom-call(bf16[33,32,256]{2,1,0:T(8,128)(2,1)S(1)} %front.2.src0.sratio0, bf16[33,64,256]{2,1,0:T(8,128)(2,1)} %collective-permute-done.src1.sratio1.chan1.cratio1, bf16[33,32,256]{2,1,0:T(8,128)(2,1)S(1)} %front.2.src0.sratio0, ...), custom_call_target="tpu_custom_call" | custom-call | flops 4294967296 | bytes 8388608 | tf_op jit(solution)/shard_map/correlate/pallas_call | solution.py:370
  59.6 0.1 collective-permute-start.3
  59.7 0.0 collective-permute-done.1
  59.8 0.1 add_convert_fusion
  59.8 3.6 %collective-permute-start.2 = (bf16[256,512]{1,0:T(8,128)(2,1)S(1)}, bf16[256,512]{1,0:T(8,128)(2,1)S(1)}, u32[]{:S(2)}, u32[]{:S(2)}) collective-permute-start(bf16[256,512]{1,0:T(8,128)(2,1)S(1)} %add_convert_fusion), channel_id=1, source_target_pairs={{0,2},{1,7},{2,4},{3,1},{4,6},{5,3},{6,0},{7,5},{8,10},{9,15},{10,... | collective-permute-start | bytes 786440 | tf_op jit(solution)/shard_map/ppermute | solution.py:459
  63.5 0.2 fusion
  63.6 0.2 convolution_maximum_fusion
  63.9 0.1 broadcast_in_dim.74
  63.9 11.5 %collective-permute-done.3.second_ref = bf16[256,512]{1,0:T(8,128)(2,1)S(1)} collective-permute-done((bf16[256,512]{1,0:T(8,128)(2,1)S(1)}, bf16[256,512]{1,0:T(8,128)(2,1)S(1)}, u32[]{:S(2)}, u32[]{:S(2)}) %collective-permute-start.3) | collective-permute-done | bytes 262176 | tf_op jit(solution)/shard_map/ppermute | solution.py:459
  75.4 0.0 collective-permute-done.2.first_ref
  75.4 0.1 broadcast_in_dim.75.count_ref
  75.5 0.9 %finish.1 = f32[256,512]{1,0:T(8,128)} custom-call(f32[256,512]{1,0:T(8,128)S(1)} %get-tuple-element.9.own_ref, bf16[256,512]{1,0:T(8,128)(2,1)S(1)} %collective-permute-done.2.first_ref, bf16[256,512]{1,0:T(8,128)(2,1)S(1)} %collective-permute-done.3.second_ref, f32[256,128]{1,0:T(8,128)S(1)} %broadcast_in_dim.75.count_ref), custom_call_target="tpu_custom_call" | custom-call | tf_op jit(solution)/shard_map/finish/pallas_call | solution.py:400
  (5 shorter events, 0.1 us)
Async XLA Ops:
  3.0 9.4 %copy-start.4 = (s32[8,1024]{1,0:T(8,128)S(1)}, s32[8,1024]{1,0:T(8,128)}, u32[]{:S(2)}) copy-start(s32[8,1024]{1,0:T(8,128)} %param.11) | copy-start | bytes 98308
  3.0 9.5 %copy-start.5 = (bf16[257]{0:T(512)(128)(2,1)S(1)}, bf16[257]{0:T(512)(128)(2,1)}, u32[]{:S(2)}) copy-start(bf16[257]{0:T(512)(128)(2,1)} %param.9) | copy-start | bytes 1546
  3.0 9.5 %copy-start = (bf16[1536,256]{1,0:T(8,128)(2,1)S(1)}, bf16[1536,256]{1,0:T(8,128)(2,1)}, u32[]{:S(2)}) copy-start(bf16[1536,256]{1,0:T(8,128)(2,1)} %constant.126.clone.rest_0_.products_ref) | copy-start | bytes 2359300
  3.0 9.5 %copy-start.1 = (f32[120,256]{1,0:T(8,128)S(1)}, f32[120,256]{1,0:T(8,128)}, u32[]{:S(2)}) copy-start(f32[120,256]{1,0:T(8,128)} %constant.127.clone.rest_1_.rotations_ref) | copy-start | bytes 368644
  3.0 9.7 %copy-start.6 = (s32[64]{0:T(128)S(1)}, s32[64]{0:T(128)}, u32[]{:S(2)}) copy-start(s32[64]{0:T(128)} %param.10) | copy-start | bytes 772
  3.0 30.2 %all-to-all-start = ((bf16[32,96,240]{2,1,0:T(8,128)(2,1)}), bf16[32,96,240]{2,1,0:T(8,128)(2,1)S(1)}, u32[]{:S(2)}, u32[]{:S(2)}) async-start(bf16[32,96,240]{2,1,0:T(8,128)(2,1)} %gather.1), calls=%async_computation | async-start | bytes 3145728 | tf_op jit(solution)/shard_map/all_to_all | solution.py:429
  39.8 5.2 %collective-permute-start = (bf16[33,64,256]{2,1,0:T(8,128)(2,1)}, bf16[33,64,256]{2,1,0:T(8,128)(2,1)}, u32[]{:S(2)}, u32[]{:S(2)}) collective-permute-start(bf16[33,64,256]{2,1,0:T(8,128)(2,1)} %front.3.chan0.cratio0), channel_id=1, source_target_pairs={{0,1},{1,0},{2,3},{3,2},{4,5},{5,4},{6,7},{7,6},{8,9},{9,8},{10,11... | collective-permute-start | bytes 3244040 | tf_op jit(solution)/shard_map/ppermute | solution.py:454
  42.1 3.0 %copy-start.2 = (bf16[32,2,128,256]{3,2,1,0:T(8,128)(2,1)S(1)}, bf16[32,2,128,256]{3,2,1,0:T(8,128)(2,1)}, u32[]{:S(2)}) copy-start(bf16[32,2,128,256]{3,2,1,0:T(8,128)(2,1)} %constant.128.clone.lags_ref) | copy-start | bytes 12582916
  42.1 3.0 %copy-start.3 = (bf16[256,256]{1,0:T(8,128)(2,1)S(1)}, bf16[256,256]{1,0:T(8,128)(2,1)}, u32[]{:S(2)}) copy-start(bf16[256,256]{1,0:T(8,128)(2,1)} %constant.129.clone.turn_ref) | copy-start | bytes 393220
  49.8 10.0 %collective-permute-start.1 = (bf16[256,512]{1,0:T(8,128)(2,1)S(1)}, bf16[256,512]{1,0:T(8,128)(2,1)S(1)}, u32[]{:S(2)}, u32[]{:S(2)}) collective-permute-start(bf16[256,512]{1,0:T(8,128)(2,1)S(1)} %get-tuple-element.11), channel_id=1, source_target_pairs={{0,2},{1,7},{2,4},{3,1},{4,6},{5,3},{6,0},{7,5},{8,10},{9,15},{10,... | collective-permute-start | bytes 786440 | tf_op jit(solution)/shard_map/ppermute | solution.py:459
  59.6 15.8 %collective-permute-start.3 = (bf16[256,512]{1,0:T(8,128)(2,1)S(1)}, bf16[256,512]{1,0:T(8,128)(2,1)S(1)}, u32[]{:S(2)}, u32[]{:S(2)}) collective-permute-start(bf16[256,512]{1,0:T(8,128)(2,1)S(1)} %get-tuple-element.12), channel_id=1, source_target_pairs={{0,6},{1,3},{2,0},{3,5},{4,2},{5,7},{6,4},{7,1},{8,14},{9,11},{10,... | collective-permute-start | bytes 786440 | tf_op jit(solution)/shard_map/ppermute | solution.py:459
  59.8 15.6 %collective-permute-start.2 = (bf16[256,512]{1,0:T(8,128)(2,1)S(1)}, bf16[256,512]{1,0:T(8,128)(2,1)S(1)}, u32[]{:S(2)}, u32[]{:S(2)}) collective-permute-start(bf16[256,512]{1,0:T(8,128)(2,1)S(1)} %add_convert_fusion), channel_id=1, source_target_pairs={{0,2},{1,7},{2,4},{3,1},{4,6},{5,3},{6,0},{7,5},{8,10},{9,15},{10,... | collective-permute-start | bytes 786440 | tf_op jit(solution)/shard_map/ppermute | solution.py:459
where the time goes:
time: 76.7 us; the launch traced here: 76.4 us
  waiting for transfers between devices  31.6 us (41%)
  Pallas kernels  22.8 us (30%)
  starting transfers between devices  20.5 us (27%)
    all_to_all x1, waiting for transfers between devices, body(): lax.all_to_all(sent, 'chan', split_axis=0, concat_axis=0, tiled=True)  20.1 us
    ppermute x3, waiting for transfers between devices, along(): lax.ppermute(values, 'tm', [(j, (j + steps[j]) % time_count) for j in ran...  11.5 us
    pallas_call x2, Pallas kernels, front(): pl.pallas_call(functools.partial(front_kernel, rotated // ROW_STEP), grid...  9.41 us
    pallas_call x2, Pallas kernels, correlate(): pl.pallas_call(correlate_kernel, grid=(steps,), in_specs=[src_spec, src_s...  9.4 us
    all_to_all x1, starting transfers between devices, body(): lax.all_to_all(sent, 'chan', split_axis=0, concat_axis=0, tiled=True)  9.36 us
    ppermute x3, starting transfers between devices, along(): lax.ppermute(values, 'tm', [(j, (j + steps[j]) % time_count) for j in ran...  8.9 us
    pallas_call x1, Pallas kernels, gather_rows(): pl.pallas_call(gather_kernel, grid=(steps,), in_specs=[pl.BlockSpec((1, t...  2.97 us
    ppermute x1, starting transfers between devices, body(): got = lax.ppermute(swap, 'tm', [(j, j ^ 1) for j in range(time_count)])  2.21 us
  transfers between devices with their start and end apart: 5, of which 2 were waited for; matrix products, arithmetic and copies ran while one was open for 1% of the time, Pallas kernels for 10%

commit v1 on v0

--- a/solution.py
+++ b/solution.py
@@ -19,7 +19,7 @@
 LAGS = 512
 TILE = 256
 STEP_K2 = 16
-ROW_STEP = 16
+ROW_STEP = 32
 ROW_PART = 8
 VMEM_LIMIT = 16 * 1024 * 1024
 PLANES = ROWS_B + 1

time: 76.7 us -> 75.5 us (0.984)
  Pallas kernels: 22.8 us -> 20.8 us
  starting transfers between devices: 20.5 us -> 22.5 us
  waiting for transfers between devices: 31.6 us -> 30.5 us
    pallas_call x2, Pallas kernels: 9.41 us -> 7.42 us  [front(): pl.pallas_call(functools.partial(front_kernel, rotated // ROW_STEP), grid...]
    ppermute x3, starting transfers between devices: 8.9 us -> 10.9 us  [along(): lax.ppermute(values, 'tm', [(j, (j + steps[j]) % time_count) for j in ran...]
    ppermute x3, waiting for transfers between devices: 11.5 us -> 10 us  [along(): lax.ppermute(values, 'tm', [(j, (j + steps[j]) % time_count) for j in ran...]
  transfers between devices with their start and end apart: 5 -> 5, of which waited for: 2 -> 3; matrix products, arithmetic and copies ran while one was open for 1% -> 1% of each run, Pallas kernels for 10% -> 9%
where the time goes in v1:
time: 75.5 us; the launch traced here: 75.3 us
  waiting for transfers between devices  30.5 us (40%)
  starting transfers between devices  22.5 us (30%)
  Pallas kernels  20.8 us (28%)
    all_to_all x1, waiting for transfers between devices, body(): lax.all_to_all(sent, 'chan', split_axis=0, concat_axis=0, tiled=True)  20.1 us
    ppermute x3, starting transfers between devices, along(): lax.ppermute(values, 'tm', [(j, (j + steps[j]) % time_count) for j in ran...  10.9 us
    ppermute x3, waiting for transfers between devices, along(): lax.ppermute(values, 'tm', [(j, (j + steps[j]) % time_count) for j in ran...  10 us
    pallas_call x2, Pallas kernels, correlate(): pl.pallas_call(correlate_kernel, grid=(steps,), in_specs=[src_spec, src_s...  9.39 us
    all_to_all x1, starting transfers between devices, body(): lax.all_to_all(sent, 'chan', split_axis=0, concat_axis=0, tiled=True)  9.37 us
    pallas_call x2, Pallas kernels, front(): pl.pallas_call(functools.partial(front_kernel, rotated // ROW_STEP), grid...  7.42 us
    pallas_call x1, Pallas kernels, gather_rows(): pl.pallas_call(gather_kernel, grid=(steps,), in_specs=[pl.BlockSpec((1, t...  2.96 us
    ppermute x1, starting transfers between devices, body(): got = lax.ppermute(swap, 'tm', [(j, j ^ 1) for j in range(time_count)])  2.24 us
  transfers between devices with their start and end apart: 5, of which 3 were waited for; matrix products, arithmetic and copies ran while one was open for 1% of the time, Pallas kernels for 9%

profile of v1, /device:TPU:1, one launch (start us, length us, event | category | flops | bytes accessed | tf_op | source)
XLA Modules:
  0.0 75.3 jit_solution(1173165600857995010)
XLA Ops:
  0.0 3.0 %gather.1 = bf16[32,96,240]{2,1,0:T(8,128)(2,1)} custom-call(s32[1,64]{1,0:T(1,128)} %bitcast.11, bf16[240,1024]{1,0:T(8,128)(2,1)} %bitcast.9), custom_call_target="tpu_custom_call" | custom-call | tf_op jit(solution)/shard_map/gather/pallas_call | solution.py:148
  3.0 0.0 copy-start.4
  3.0 0.0 copy-start.5
  3.0 0.0 copy-start
  3.0 0.0 copy-start.1
  3.0 0.0 copy-start.6
  3.0 9.4 %all-to-all-start = ((bf16[32,96,240]{2,1,0:T(8,128)(2,1)}), bf16[32,96,240]{2,1,0:T(8,128)(2,1)S(1)}, u32[]{:S(2)}, u32[]{:S(2)}) async-start(bf16[32,96,240]{2,1,0:T(8,128)(2,1)} %gather.1), calls=%async_computation | async-start | bytes 3145728 | tf_op jit(solution)/shard_map/all_to_all | solution.py:429
  12.4 0.0 copy-done.4
  12.4 0.0 copy-done.5
  12.5 0.0 copy-done
  12.5 0.0 copy-done.1
  12.5 0.1 toeplitz.1.toeplitz_ref
  12.6 0.0 copy-done.6
  12.6 0.2 select_reduce_fusion.1
  12.8 0.1 pad_add_fusion
  12.9 0.2 select_reduce_fusion
  13.1 20.1 %all-to-all-done.pieces_ref = bf16[32,96,240]{2,1,0:T(8,128)(2,1)S(1)} async-done(((bf16[32,96,240]{2,1,0:T(8,128)(2,1)}), bf16[32,96,240]{2,1,0:T(8,128)(2,1)S(1)}, u32[]{:S(2)}, u32[]{:S(2)}) %all-to-all-start) | async-done | bytes 1474592 | tf_op jit(solution)/shard_map/all_to_all | solution.py:429
  33.2 0.1 broadcast_in_dim.73.mask_ref
  33.3 5.2 %front.3.chan0.cratio0 = bf16[33,64,256]{2,1,0:T(8,128)(2,1)} custom-call(bf16[32,96,240]{2,1,0:T(8,128)(2,1)S(1)} %all-to-all-done.pieces_ref, bf16[512,256]{1,0:T(8,128)(2,1)S(1)} %toeplitz.1.toeplitz_ref, bf16[1536,256]{1,0:T(8,128)(2,1)S(1)} %copy-done, f32[120,256]{1,0:T(8,128)S(1)} %copy-done.1, f32[96,128]{1,0:T(8,128)S(1)} %broadcast_in_dim.73.mask_ref), custom_call_target="tpu_custom_call" | custom-call | flops 7040000000 | bytes 4000000 | tf_op jit(solution)/shard_map/front/pallas_call | solution.py:255
  38.5 2.2 %collective-permute-start = (bf16[33,64,256]{2,1,0:T(8,128)(2,1)}, bf16[33,64,256]{2,1,0:T(8,128)(2,1)}, u32[]{:S(2)}, u32[]{:S(2)}) collective-permute-start(bf16[33,64,256]{2,1,0:T(8,128)(2,1)} %front.3.chan0.cratio0), channel_id=1, source_target_pairs={{0,1},{1,0},{2,3},{3,2},{4,5},{5,4},{6,7},{7,6},{8,9},{9,8},{10,11... | collective-permute-start | bytes 3244040 | tf_op jit(solution)/shard_map/ppermute | solution.py:454
  40.7 0.1 dynamic_slice.11
  40.8 0.0 copy-start.2
  40.8 0.0 copy-start.3
  40.8 2.2 %front.2.src0.sratio0 = bf16[33,32,256]{2,1,0:T(8,128)(2,1)S(1)} custom-call(bf16[32,96,240]{2,1,0:T(8,128)(2,1)S(1)} %all-to-all-done.pieces_ref, bf16[512,256]{1,0:T(8,128)(2,1)S(1)} %toeplitz.1.toeplitz_ref, bf16[1536,256]{1,0:T(8,128)(2,1)S(1)} %copy-done, f32[120,256]{1,0:T(8,128)S(1)} %copy-done.1, f32[96,128]{1,0:T(8,128)S(1)} %broadcast_in_dim.73.mask_ref), custom_call_target="tpu_custom_call" | custom-call | flops 3520000000 | bytes 4000000 | tf_op jit(solution)/shard_map/front/pallas_call | solution.py:255
  43.0 0.4 collective-permute-done.src1.sratio1.chan1.cratio1
  43.4 0.0 copy-done.2
  43.4 0.0 copy-done.3
  43.4 4.7 %correlate.3 = (bf16[256,512]{1,0:T(8,128)(2,1)S(1)}, f32[256,512]{1,0:T(8,128)S(1)}) custom-call(bf16[33,32,256]{2,1,0:T(8,128)(2,1)S(1)} %front.2.src0.sratio0, bf16[33,64,256]{2,1,0:T(8,128)(2,1)} %collective-permute-done.src1.sratio1.chan1.cratio1, bf16[33,32,256]{2,1,0:T(8,128)(2,1)S(1)} %front.2.src0.sratio0, ...), custom_call_target="tpu_custom_call" | custom-call | flops 4294967296 | bytes 8388608 | tf_op jit(solution)/shard_map/correlate/pallas_call | solution.py:370
  48.1 5.4 %collective-permute-start.1 = (bf16[256,512]{1,0:T(8,128)(2,1)S(1)}, bf16[256,512]{1,0:T(8,128)(2,1)S(1)}, u32[]{:S(2)}, u32[]{:S(2)}) collective-permute-start(bf16[256,512]{1,0:T(8,128)(2,1)S(1)} %get-tuple-element.11), channel_id=1, source_target_pairs={{0,2},{1,7},{2,4},{3,1},{4,6},{5,3},{6,0},{7,5},{8,10},{9,15},{10,... | collective-permute-start | bytes 786440 | tf_op jit(solution)/shard_map/ppermute | solution.py:459
  53.5 4.7 %correlate.2 = (bf16[256,512]{1,0:T(8,128)(2,1)S(1)}, f32[256,512]{1,0:T(8,128)S(1)}) custom-call(bf16[33,32,256]{2,1,0:T(8,128)(2,1)S(1)} %front.2.src0.sratio0, bf16[33,64,256]{2,1,0:T(8,128)(2,1)} %collective-permute-done.src1.sratio1.chan1.cratio1, bf16[33,32,256]{2,1,0:T(8,128)(2,1)S(1)} %front.2.src0.sratio0, ...), custom_call_target="tpu_custom_call" | custom-call | flops 4294967296 | bytes 8388608 | tf_op jit(solution)/shard_map/correlate/pallas_call | solution.py:370
  58.2 0.1 collective-permute-start.3
  58.3 0.0 collective-permute-done.1
  58.3 0.1 add_convert_fusion
  58.4 5.4 %collective-permute-start.2 = (bf16[256,512]{1,0:T(8,128)(2,1)S(1)}, bf16[256,512]{1,0:T(8,128)(2,1)S(1)}, u32[]{:S(2)}, u32[]{:S(2)}) collective-permute-start(bf16[256,512]{1,0:T(8,128)(2,1)S(1)} %add_convert_fusion), channel_id=1, source_target_pairs={{0,2},{1,7},{2,4},{3,1},{4,6},{5,3},{6,0},{7,5},{8,10},{9,15},{10,... | collective-permute-start | bytes 786440 | tf_op jit(solution)/shard_map/ppermute | solution.py:459
  63.8 0.2 fusion
  64.0 0.2 convolution_maximum_fusion
  64.2 0.1 broadcast_in_dim.74
  64.3 10.0 %collective-permute-done.3.second_ref = bf16[256,512]{1,0:T(8,128)(2,1)S(1)} collective-permute-done((bf16[256,512]{1,0:T(8,128)(2,1)S(1)}, bf16[256,512]{1,0:T(8,128)(2,1)S(1)}, u32[]{:S(2)}, u32[]{:S(2)}) %collective-permute-start.3) | collective-permute-done | bytes 262176 | tf_op jit(solution)/shard_map/ppermute | solution.py:459
  74.3 0.0 collective-permute-done.2.first_ref
  74.3 0.1 broadcast_in_dim.75.count_ref
  74.4 0.9 %finish.1 = f32[256,512]{1,0:T(8,128)} custom-call(f32[256,512]{1,0:T(8,128)S(1)} %get-tuple-element.9.own_ref, bf16[256,512]{1,0:T(8,128)(2,1)S(1)} %collective-permute-done.2.first_ref, bf16[256,512]{1,0:T(8,128)(2,1)S(1)} %collective-permute-done.3.second_ref, f32[256,128]{1,0:T(8,128)S(1)} %broadcast_in_dim.75.count_ref), custom_call_target="tpu_custom_call" | custom-call | tf_op jit(solution)/shard_map/finish/pallas_call | solution.py:400
  (5 shorter events, 0.1 us)
Async XLA Ops:
  3.0 9.4 %copy-start.4 = (s32[8,1024]{1,0:T(8,128)S(1)}, s32[8,1024]{1,0:T(8,128)}, u32[]{:S(2)}) copy-start(s32[8,1024]{1,0:T(8,128)} %param.11) | copy-start | bytes 98308
  3.0 9.5 %copy-start.5 = (bf16[257]{0:T(512)(128)(2,1)S(1)}, bf16[257]{0:T(512)(128)(2,1)}, u32[]{:S(2)}) copy-start(bf16[257]{0:T(512)(128)(2,1)} %param.9) | copy-start | bytes 1546
  3.0 9.5 %copy-start = (bf16[1536,256]{1,0:T(8,128)(2,1)S(1)}, bf16[1536,256]{1,0:T(8,128)(2,1)}, u32[]{:S(2)}) copy-start(bf16[1536,256]{1,0:T(8,128)(2,1)} %constant.126.clone.rest_0_.products_ref) | copy-start | bytes 2359300
  3.0 9.5 %copy-start.1 = (f32[120,256]{1,0:T(8,128)S(1)}, f32[120,256]{1,0:T(8,128)}, u32[]{:S(2)}) copy-start(f32[120,256]{1,0:T(8,128)} %constant.127.clone.rest_1_.rotations_ref) | copy-start | bytes 368644
  3.0 9.7 %copy-start.6 = (s32[64]{0:T(128)S(1)}, s32[64]{0:T(128)}, u32[]{:S(2)}) copy-start(s32[64]{0:T(128)} %param.10) | copy-start | bytes 772
  3.0 30.2 %all-to-all-start = ((bf16[32,96,240]{2,1,0:T(8,128)(2,1)}), bf16[32,96,240]{2,1,0:T(8,128)(2,1)S(1)}, u32[]{:S(2)}, u32[]{:S(2)}) async-start(bf16[32,96,240]{2,1,0:T(8,128)(2,1)} %gather.1), calls=%async_computation | async-start | bytes 3145728 | tf_op jit(solution)/shard_map/all_to_all | solution.py:429
  38.5 4.9 %collective-permute-start = (bf16[33,64,256]{2,1,0:T(8,128)(2,1)}, bf16[33,64,256]{2,1,0:T(8,128)(2,1)}, u32[]{:S(2)}, u32[]{:S(2)}) collective-permute-start(bf16[33,64,256]{2,1,0:T(8,128)(2,1)} %front.3.chan0.cratio0), channel_id=1, source_target_pairs={{0,1},{1,0},{2,3},{3,2},{4,5},{5,4},{6,7},{7,6},{8,9},{9,8},{10,11... | collective-permute-start | bytes 3244040 | tf_op jit(solution)/shard_map/ppermute | solution.py:454
  40.8 2.6 %copy-start.2 = (bf16[32,2,128,256]{3,2,1,0:T(8,128)(2,1)S(1)}, bf16[32,2,128,256]{3,2,1,0:T(8,128)(2,1)}, u32[]{:S(2)}) copy-start(bf16[32,2,128,256]{3,2,1,0:T(8,128)(2,1)} %constant.128.clone.lags_ref) | copy-start | bytes 12582916
  40.8 2.6 %copy-start.3 = (bf16[256,256]{1,0:T(8,128)(2,1)S(1)}, bf16[256,256]{1,0:T(8,128)(2,1)}, u32[]{:S(2)}) copy-start(bf16[256,256]{1,0:T(8,128)(2,1)} %constant.129.clone.turn_ref) | copy-start | bytes 393220
  48.1 10.1 %collective-permute-start.1 = (bf16[256,512]{1,0:T(8,128)(2,1)S(1)}, bf16[256,512]{1,0:T(8,128)(2,1)S(1)}, u32[]{:S(2)}, u32[]{:S(2)}) collective-permute-start(bf16[256,512]{1,0:T(8,128)(2,1)S(1)} %get-tuple-element.11), channel_id=1, source_target_pairs={{0,2},{1,7},{2,4},{3,1},{4,6},{5,3},{6,0},{7,5},{8,10},{9,15},{10,... | collective-permute-start | bytes 786440 | tf_op jit(solution)/shard_map/ppermute | solution.py:459
  58.2 16.1 %collective-permute-start.3 = (bf16[256,512]{1,0:T(8,128)(2,1)S(1)}, bf16[256,512]{1,0:T(8,128)(2,1)S(1)}, u32[]{:S(2)}, u32[]{:S(2)}) collective-permute-start(bf16[256,512]{1,0:T(8,128)(2,1)S(1)} %get-tuple-element.12), channel_id=1, source_target_pairs={{0,6},{1,3},{2,0},{3,5},{4,2},{5,7},{6,4},{7,1},{8,14},{9,11},{10,... | collective-permute-start | bytes 786440 | tf_op jit(solution)/shard_map/ppermute | solution.py:459
  58.4 15.9 %collective-permute-start.2 = (bf16[256,512]{1,0:T(8,128)(2,1)S(1)}, bf16[256,512]{1,0:T(8,128)(2,1)S(1)}, u32[]{:S(2)}, u32[]{:S(2)}) collective-permute-start(bf16[256,512]{1,0:T(8,128)(2,1)S(1)} %add_convert_fusion), channel_id=1, source_target_pairs={{0,2},{1,7},{2,4},{3,1},{4,6},{5,3},{6,0},{7,5},{8,10},{9,15},{10,... | collective-permute-start | bytes 786440 | tf_op jit(solution)/shard_map/ppermute | solution.py:459
